TPU v7x, 32 devices: a whole 2x2x4 slice. The times are simulated.
32 devices in a mesh: occ: 8 (over y, x, core), grp: 4 (over z).
Axes of the slice: x: 2, y: 2, z: 4, core: 2. Of those that a mesh axis runs over, the one named last changes fastest.
Arguments:
- slabs: float32 [32, 512, 1024], P(('occ', 'grp')), may hold values from -1.2 to 1.2
- occ_energy: float32 [32], replicated, may hold values from -1.5 to -0.3
- vir_energy: float32 [512], replicated, may hold values from 0.1 to 3
- pair_mask: int32 [32, 2], replicated, may hold values from 0 to 1, as said below
Outputs:
- aux_grad: float32 [32, 512, 1024], P(('occ', 'grp'))
- vir_density: float32 [512, 512], P('occ')
Inputs may be any that keep to these rules, and one draw needn't show every extreme that they name: Entries are 0 or 1; orbital 0 is paired with all of its 2 partners, and so is every orbital i >= 32 - 1 - 2 (pair_mask[i, k - 1] = 1 for every 1 <= k <= 2 on those rows).
All inputs are finite; a program needn't handle non-finite values.
Results may differ from a plain program's by a relative error of at most 0.0003.
Values sent between devices are 32-bit elements; how exact they have to be, the bound alone decides.
No kernel may reach another device: no remote copies, remote signals or barrier semaphores. Data moves between devices by JAX's collectives and lax.ppermute only.
A program may use at most 128 MiB of HBM per device.

v0:
```python
import functools

import jax
import jax.numpy as jnp
from jax import lax
from jax.experimental import pallas as pl
from jax.experimental.pallas import tpu as pltpu
from jax.sharding import PartitionSpec as P

AXES = ("occ", "grp")
PIECES = 4
VMEM_LIMIT = 63 * 1024 * 1024

SMEM = pl.BlockSpec(memory_space=pltpu.SMEM)
VMEM = pl.BlockSpec(memory_space=pltpu.VMEM)
ANY = pl.BlockSpec(memory_space=pl.ANY)


def plan(nocc):
    names = ("early2", "late0", "early0", "late2", "early_p3", "to_early", "to_late", "early_home", "late_home", "before")
    routes = {name: [] for name in names}

    def both(name, source, target):
        routes[name].append(tuple(4 * block + place for block, place in (source, target)))
        routes[name].append(tuple(4 * (nocc - 1 - block) + 3 - place for block, place in (source, target)))

    for even in range(0, nocc, 2):
        odd = even + 1
        both("early2", (odd, 2), (odd, 1))
        both("late0", (even, 0), (even, 1))
        both("early0", (odd, 0), (odd, 1))
        both("late2", (even, 2), (even, 1))
        both("early_p3", (even, 3), (odd, 1))
        both("to_early", (even, 1), (odd, 1))
        both("to_late", (odd, 1), (even, 1))
        both("early_home", (odd, 1), (odd, 0))
        both("late_home", (even, 1), (even, 0))
        if even:
            both("before", (even - 1, 1), (even, 1))
    return routes


def move(block, route):
    return lax.ppermute(block, AXES, route)


def tied(x, *earlier):
    return lax.optimization_barrier((x, *earlier))[0]


class Place:
    def __init__(self, nocc, energy_ref, mask_ref):
        occ, grp = lax.axis_index("occ"), lax.axis_index("grp")
        self.energy_ref, self.mask_ref = energy_ref, mask_ref
        self.last = nocc * 4 - 1
        self.own = occ * 4 + grp
        self.lower = grp <= 1
        hub = (grp == 1) | (grp == 2)
        inner = (lax.rem(occ, 2) == 1) == self.lower
        self.early, self.late = hub & inner, hub & ~inner
        self.from_late, self.from_early = ~hub & ~inner, ~hub & inner
        step = jnp.where(self.lower, 1, -1)
        a0 = occ * 4 + jnp.where(self.lower, 0, 3)
        self.index = {"a0": a0, "a1": a0 + step, "a2": a0 + 2 * step, "a3": a0 + 3 * step, "p3": a0 - step, "p2": a0 - 2 * step}

    def pair(self, x, y):
        offset = {"a0a1": 1, "a0a2": 2, "a1a2": 1, "a1a3": 2, "a0p2": 2, "a0p3": 1, "a1p3": 2}[x + y]
        i, j = self.index[x], self.index[y]
        there = (j >= 0) & (j <= self.last)
        i, j = jnp.clip(i, 0, self.last), jnp.clip(j, 0, self.last)
        active = there & (self.mask_ref[jnp.minimum(i, j), offset - 1] == 1)
        return active, self.energy_ref[i] + self.energy_ref[j]


ROWS = ((1,), (1,))
PLAIN = ((1,), (0,))
COLUMNS = ((0,), (0,))


def mul(left, right, dims):
    return lax.dot_general(left, right, (dims, ((), ())), preferred_element_type=jnp.float32)


def halves(x):
    high = x.astype(jnp.bfloat16)
    return high, (x - high.astype(jnp.float32)).astype(jnp.bfloat16)


def parts(x, other, axis):
    high, low = halves(x)
    return jnp.concatenate([high, low, high] if other else [high, high, low], axis)


def half_squares(t):
    high, low = halves(t)
    left, right = [high, high], [high * 0.5, low]
    return mul(jnp.concatenate(left, 1), jnp.concatenate(right, 1), ROWS) + mul(
        jnp.concatenate(left, 0), jnp.concatenate(right, 0), COLUMNS
    )


def home_kernel(nocc, energy_ref, mask_ref, vir_ref, slab_ref, grad_ref, density_ref, levels_ref):
    rows = slab_ref.shape[0]
    spread = jnp.broadcast_to(vir_ref[...], (rows, rows))
    levels_ref[...] = spread + spread.T
    energy = energy_ref[Place(nocc, energy_ref, mask_ref).own]
    slab = slab_ref[...]
    t = mul(parts(slab, False, 1), parts(slab, True, 1), ROWS) / (2.0 * energy - levels_ref[...])
    t3 = parts(t, False, 1)
    grad_ref[...] = 2.0 * mul(t3, parts(slab, True, 0), PLAIN)
    density_ref[...] = mul(t3, parts(t, True, 1), ROWS)


def slots_of(tasks):
    found = {}
    for role, x, y, *_ in tasks:
        for orbital in (x, y):
            name = "own" if orbital == "a1" else role + orbital[1:] if orbital[0] == "a" else role + "_" + orbital
            if name not in found.setdefault(role, {}):
                found[role][name] = (len(found[role]), orbital)
    return found


def pairs_kernel(nocc, tasks, names, given, made, fresh, energy_ref, mask_ref, levels_ref, *refs):
    slabs, refs = dict(zip(names, refs[:len(names)])), refs[len(names):]
    before, refs = dict(zip(given, refs[:len(given)])), refs[len(given):]
    after, refs = dict(zip(made, refs[:len(made)])), refs[len(made):]
    slots, split, slabs_sem, sums, square, levels, t_ref, sums_sem, meta, energies, state = refs
    width = slots.shape[2]
    place = Place(nocc, energy_ref, mask_ref)
    roles = {"early": place.early, "late": place.late}
    layout = slots_of(tasks)
    added = {name: jnp.bool_(False) for name in ("g0", "g1", "density")}
    needed = {role: [jnp.bool_(False)] * len(layout[role]) for role in layout}
    for k, (role, x, y, left, right, counted) in enumerate(tasks):
        active, energy = place.pair(x, y)
        active = active & roles[role]
        energies[k] = energy
        meta[k, 0] = active.astype(jnp.int32)
        for column, orbital in ((1, x), (2, y)):
            slot = next(slot for slot, held in layout[role].values() if held == orbital)
            meta[k, column] = slot
            needed[role][slot] = needed[role][slot] | active
        meta[k, 3] = ("", "g0", "g1").index(left)
        meta[k, 4] = ("", "g0", "g1").index(right)
        counts = place.lower if counted == "lower" else jnp.bool_(bool(counted))
        for name, used in ((left, active), (right, active), ("density", active & counts)):
            if name:
                added[name] = added[name] | used
        meta[k, 5] = counts.astype(jnp.int32)
    run = functools.reduce(jnp.logical_or, [roles[role] for role in layout])
    held = {"g0": sums.at[0], "g1": sums.at[1], "density": square}
    uses = {name: run if name in fresh or name not in given else added[name] for name in made}

    def wanted(name, copies):
        @pl.when(uses[name])
        def _():
            copies(name)

    @pl.when(run)
    def _():
        state[0] = 0
        for s in range(slots.shape[0]):
            meta[s, 6] = 0
        for role in layout:
            for name, (s, _) in layout[role].items():

                @pl.when(needed[role][s])
                def _():
                    meta[s, 6] = 1
                    pltpu.make_async_copy(slabs[name], slots.at[s], slabs_sem.at[s]).start()

        pltpu.make_async_copy(levels_ref, levels, sums_sem.at[0]).start()
        for q, name in enumerate(given):
            wanted(name, lambda name: pltpu.make_async_copy(before[name], held[name], sums_sem.at[q + 1]).start())
        if "g0" in made and "g0" not in given:
            sums[0] = jnp.zeros(sums.shape[1:], sums.dtype)

        def arrived():
            @pl.when(state[0] == 0)
            def _():
                pltpu.make_async_copy(levels_ref, levels, sums_sem.at[0]).wait()
                for q, name in enumerate(given):
                    wanted(name, lambda name: pltpu.make_async_copy(before[name], held[name], sums_sem.at[q + 1]).wait())
                state[0] = 1

        @pl.loop(0, len(tasks))
        def _(k):
            @pl.when(meta[k, 0] == 1)
            def _():
                @pl.loop(1, 3)
                def _(column):
                    s = meta[k, column]

                    @pl.when(meta[s, 6] == 1)
                    def _():
                        pltpu.make_async_copy(slabs[names[0]], slots.at[s], slabs_sem.at[s]).wait()
                        high, low = halves(slots[s])
                        split[s, :, 0:width] = high
                        split[s, :, width:2 * width] = low
                        split[s, :, 2 * width:3 * width] = high
                        meta[s, 6] = 0

                x, y = split.at[meta[k, 1]], split.at[meta[k, 2]]
                t_ref[...] = mul(x[:, width:], y[:, :2 * width], ROWS) + mul(x[:, :width], y[:, :width], ROWS)
                arrived()
                t = t_ref[...] / (energies[k] - levels[...])
                t_ref[...] = t
                high, low = halves(t)

                def onto(target, z, dims):
                    wide = mul(high, z[:, :2 * width], dims)
                    sums[target] += wide[:, :width] + wide[:, width:] + mul(low, z[:, :width], dims)

                if any(task[3] for task in tasks):

                    @pl.when(meta[k, 3] > 0)
                    def _():
                        onto(meta[k, 3] - 1, y, PLAIN)

                if any(task[4] for task in tasks):

                    @pl.when(meta[k, 4] > 0)
                    def _():
                        onto(meta[k, 4] - 1, x, COLUMNS)

                if any(task[5] for task in tasks):

                    @pl.when(meta[k, 5] == 1)
                    def _():
                        square[...] += half_squares(t_ref[...])

        arrived()
        for q, name in enumerate(made):
            wanted(name, lambda name: pltpu.make_async_copy(held[name], after[name], sums_sem.at[q]).start())
        for q, name in enumerate(made):
            wanted(name, lambda name: pltpu.make_async_copy(held[name], after[name], sums_sem.at[q]).wait())


def count_kernel(density_ref, out_ref):
    total = density_ref[...]
    out_ref[...] = total + total.T


def home_sum_kernel(nocc, energy_ref, mask_ref, own_ref, late_ref, early_ref, out_ref, slots, own_sem, sum_sem, out_sem):
    place = Place(nocc, energy_ref, mask_ref)
    step = own_ref.shape[0] // PIECES

    def add(source):
        pieces = [pl.ds(p * step, step) for p in range(PIECES)]

        def own(p):
            return pltpu.make_async_copy(own_ref.at[pieces[p]], slots.at[0, pieces[p]], own_sem.at[p])

        def other(p):
            return pltpu.make_async_copy(source.at[pieces[p]], slots.at[1, pieces[p]], sum_sem.at[p])

        def out(p):
            return pltpu.make_async_copy(slots.at[0, pieces[p]], out_ref.at[pieces[p]], out_sem.at[p])

        for p in range(PIECES):
            own(p).start()
            other(p).start()
        for p in range(PIECES):
            own(p).wait()
            other(p).wait()
            slots[0, pieces[p]] += slots[1, pieces[p]]
            out(p).start()
        for p in range(PIECES):
            out(p).wait()

    @pl.when(place.from_late)
    def _():
        add(late_ref)

    @pl.when(place.from_early)
    def _():
        add(early_ref)


def body(slabs, occ_energy, vir_energy, pair_mask):
    nocc, ngrp = lax.axis_size("occ"), lax.axis_size("grp")
    routes = plan(nocc)
    own = slabs[0]
    rows, width = own.shape
    slab = jax.ShapeDtypeStruct((rows, width), jnp.float32)
    square = jax.ShapeDtypeStruct((rows, rows), jnp.float32)
    shapes = {"g0": slab, "g1": slab, "density": square}
    cost = pl.CostEstimate(flops=1000, bytes_accessed=1000, transcendentals=0)
    params = pltpu.CompilerParams(vmem_limit_bytes=VMEM_LIMIT)

    def pairs(tasks, there, given, made, fresh=()):
        inputs = [levels, *there.values(), *given.values()]
        first = 2 + len(inputs) - len(given)
        count = max(len(held) for held in slots_of(tasks).values())
        return pl.pallas_call(
            functools.partial(pairs_kernel, nocc, tasks, list(there), list(given), made, fresh),
            out_shape=[shapes[name] for name in made],
            in_specs=[SMEM, SMEM] + [ANY] * len(inputs),
            out_specs=[ANY] * len(made),
            scratch_shapes=[
                pltpu.VMEM((count, rows, width), jnp.float32),
                pltpu.VMEM((count, rows, 3 * width), jnp.bfloat16),
                pltpu.SemaphoreType.DMA((count,)),
                pltpu.VMEM((2, rows, width), jnp.float32),
                pltpu.VMEM((rows, rows), jnp.float32),
                pltpu.VMEM((rows, rows), jnp.float32),
                pltpu.VMEM((rows, rows), jnp.float32),
                pltpu.SemaphoreType.DMA((4,)),
                pltpu.SMEM((max(len(tasks), count), 8), jnp.int32),
                pltpu.SMEM((len(tasks),), jnp.float32),
                pltpu.SMEM((1,), jnp.int32),
            ],
            input_output_aliases={first + q: made.index(n) for q, n in enumerate(given) if n not in fresh},
            compiler_params=params,
            cost_estimate=cost,
            name="pairs",
        )(occ_energy, pair_mask, *inputs)

    early2 = move(own, routes["early2"])
    late0 = move(own, routes["late0"])
    home_grad, home_density, levels = pl.pallas_call(
        functools.partial(home_kernel, nocc),
        out_shape=[slab, square, square],
        in_specs=[SMEM, SMEM, VMEM, VMEM],
        out_specs=[VMEM] * 3,
        compiler_params=params,
        cost_estimate=cost,
        name="home_pair",
    )(occ_energy, pair_mask, vir_energy.reshape(1, rows), own)
    late0 = tied(late0, home_density)
    early3 = move(late0, routes["early2"])
    early0 = move(tied(own, late0), routes["early0"])
    late_p2 = move(tied(early2, home_density), routes["before"])
    g0, g1, density = pairs(
        [("early", "a1", "a2", "g1", "", "all"), ("late", "a0", "a1", "g0", "g1", "all")],
        {"own": own, "early2": early2, "late0": late0},
        {"g1": home_grad, "density": home_density},
        ["g0", "g1", "density"],
    )
    early3 = tied(early3, g1)
    late2 = move(tied(own, early3), routes["late2"])
    late_p3 = move(early3, routes["before"])
    g0, g1, density = pairs(
        [
            ("early", "a1", "a3", "g1", "", "all"),
            ("early", "a0", "a1", "g0", "g1", "all"),
            ("late", "a0", "p2", "g0", "", "all"),
        ],
        {"own": own, "early0": early0, "early3": early3, "late0": late0, "late_p2": late_p2},
        {"g0": g0, "g1": g1, "density": density},
        ["g0", "g1", "density"],
    )
    early_p3 = move(tied(own, g1), routes["early_p3"])
    late2 = tied(late2, g1)
    early_p2 = move(late2, routes["to_early"])
    g0, density = pairs(
        [
            ("early", "a0", "a2", "g0", "", "all"),
            ("early", "a0", "p2", "g0", "", "all"),
            ("late", "a0", "a2", "g0", "", ""),
            ("late", "a0", "p3", "g0", "", "lower"),
        ],
        {
            "early0": early0, "early2": early2, "early_p2": early_p2, "late0": late0, "late2": late2,
            "late_p3": tied(late_p3, g1),
        },
        {"g0": g0, "density": density},
        ["g0", "density"],
    )
    late_home = move(g0, routes["late_home"])
    (g1,) = pairs(
        [("late", "a1", "a2", "g1", "", ""), ("late", "a1", "p3", "g1", "", "")],
        {"own": own, "late2": late2, "late_p3": late_p3},
        {"g1": tied(g1, g0)},
        ["g1"],
    )
    early_p3 = tied(early_p3, g1)
    g0, density = pairs(
        [("early", "a0", "p3", "g0", "", "lower")],
        {"early0": early0, "early_p3": early_p3},
        {"g0": g0, "density": density},
        ["g0", "density"],
        fresh=("g0",),
    )
    early_home = move(g0, routes["early_home"])
    late3 = move(tied(early_p3, g0), routes["to_late"])
    density = pl.pallas_call(
        count_kernel, out_shape=square, compiler_params=params, cost_estimate=cost, name="count"
    )(density)

    def meanwhile(earlier):
        (grad,) = pairs(
            [("early", "a1", "p3", "g1", "", "")], {"own": own, "early_p3": early_p3}, {"g1": tied(g1, earlier)}, ["g1"]
        )
        grad = pl.pallas_call(
            functools.partial(home_sum_kernel, nocc),
            out_shape=slab,
            in_specs=[SMEM, SMEM, ANY, ANY, ANY],
            out_specs=ANY,
            scratch_shapes=[
                pltpu.VMEM((2, rows, width), jnp.float32),
                pltpu.SemaphoreType.DMA((PIECES,)),
                pltpu.SemaphoreType.DMA((PIECES,)),
                pltpu.SemaphoreType.DMA((PIECES,)),
            ],
            input_output_aliases={2: 0},
            compiler_params=params,
            cost_estimate=cost,
            name="home_sum",
        )(occ_energy, pair_mask, grad, late_home, early_home)
        return pairs([("late", "a1", "a3", "g1", "", "")], {"own": own, "late3": late3}, {"g1": grad}, ["g1"])[0]

    blocks, gradient = reduced(density, nocc, ngrp, meanwhile, late_home)
    return gradient[None], blocks / (nocc * ngrp)


def combined(parts):
    while len(parts) > 1:
        parts = [x + y for x, y in zip(parts[::2], parts[1::2])]
    return parts[0]


def reduced(density, nocc, ngrp, meanwhile, arriving):
    place = lax.axis_index("occ")
    width = density.shape[1]
    rows = density.shape[0] // nocc
    blocks = density
    bit, radix = 1, 2
    while bit < nocc:
        radix = min(radix, nocc // bit)
        blocks = blocks.reshape(-1, radix, rows, width)
        digit = (place // bit) % radix
        received = []
        for j in range(radix):
            part = lax.dynamic_index_in_dim(blocks, digit ^ j, 1, keepdims=False)
            if j:
                part = lax.ppermute(part, "occ", [(o, o ^ (j * bit)) for o in range(nocc)])
            received.append(part)
        blocks = combined(received)
        bit, radix = bit * radix, 4
    blocks = tied(blocks.reshape(rows, width), arriving)
    others = [lax.ppermute(blocks, "grp", [(g, g ^ j) for g in range(ngrp)]) for j in range(1, ngrp)]
    made = meanwhile(blocks)
    others = lax.optimization_barrier((*others, made))[:-1]
    return combined([blocks, *others]), made


def solution(mesh):
    nocc = mesh.shape["occ"]
    if mesh.shape["grp"] != 4 or nocc < 4 or nocc & (nocc - 1):
        raise NotImplementedError("another mesh")
    placed = (P(AXES, None, None), P(), P(), P())
    return jax.shard_map(
        body,
        mesh=mesh,
        in_specs=placed,
        out_specs=(P(AXES, None, None), P("occ", None)),
        check_vma=False,
    )
```

profile of v0, /device:TPU:0, one launch (start us, length us, event | category | flops | bytes accessed | tf_op | source)
XLA Modules:
  0.0 158.9 jit_solution(5366716448445985796)
XLA Ops:
  0.6 6.3 %collective-permute-start = (f32[512,1024]{1,0:T(8,128)}, f32[512,1024]{1,0:T(8,128)}, u32[]{:S(2)}, u32[]{:S(2)}) collective-permute-start(f32[512,1024]{1,0:T(8,128)} %bitcast.10), channel_id=1, source_target_pairs={{0,1},{31,30},{8,9},{23,22},{16,17},{15,14},{24,25},{7,6}} | collective-permute-start | bytes 6291464 | tf_op jit(solution)/shard_map/ppermute | solution.py:44
  6.9 2.0 %collective-permute-start.3 = (f32[512,1024]{1,0:T(8,128)}, f32[512,1024]{1,0:T(8,128)}, u32[]{:S(2)}, u32[]{:S(2)}) collective-permute-start(f32[512,1024]{1,0:T(8,128)} %bitcast.11), channel_id=1, source_target_pairs={{6,5},{25,26},{14,13},{17,18},{22,21},{9,10},{30,29},{1,2}} | collective-permute-start | bytes 6291464 | tf_op jit(solution)/shard_map/ppermute | solution.py:44
  8.9 1.4 copy.26.mask_ref
  10.3 7.3 %home_pair.1 = (f32[512,1024]{1,0:T(8,128)}, f32[512,512]{1,0:T(8,128)}, f32[512,512]{1,0:T(8,128)}) custom-call(f32[32]{0:T(128)} %energy_ref.17, s32[32,2]{1,0:T(8,128)} %copy.26.mask_ref, f32[1,512]{1,0:T(1,128)} %bitcast.24, f32[512,1024]{1,0:T(8,128)} %bitcast.12), custom_call_target="tpu_custom_call" | custom-call | flops 1000 | bytes 1000 | tf_op jit(solution)/shard_map/home_pair/pallas_call | solution.py:322
  17.6 11.9 %collective-permute-done.refs_2_.refs_3_ = f32[512,1024]{1,0:T(8,128)} collective-permute-done((f32[512,1024]{1,0:T(8,128)}, f32[512,1024]{1,0:T(8,128)}, u32[]{:S(2)}, u32[]{:S(2)}) %collective-permute-start) | collective-permute-done | bytes 2097184 | tf_op jit(solution)/shard_map/ppermute | solution.py:44
  29.4 2.0 %collective-permute-start.2 = (f32[512,1024]{1,0:T(8,128)}, f32[512,1024]{1,0:T(8,128)}, u32[]{:S(2)}, u32[]{:S(2)}) collective-permute-start(f32[512,1024]{1,0:T(8,128)} %collective-permute-done.refs_2_.refs_3_), channel_id=1, source_target_pairs={{6,5},{25,26},{14,13},{17,18},{22,21},{9,10},{30,29},{1,2}} | collective-permute-start | bytes 6291464 | tf_op jit(solution)/shard_map/ppermute | solution.py:44
  31.4 0.0 collective-permute-done.3.refs_1_
  31.4 2.0 %collective-permute-start.1 = (f32[512,1024]{1,0:T(8,128)}, f32[512,1024]{1,0:T(8,128)}, u32[]{:S(2)}, u32[]{:S(2)}) collective-permute-start(f32[512,1024]{1,0:T(8,128)} %bitcast.13), channel_id=1, source_target_pairs={{4,5},{27,26},{12,13},{19,18},{20,21},{11,10},{28,29},{3,2}} | collective-permute-start | bytes 6291464 | tf_op jit(solution)/shard_map/ppermute | solution.py:44
  33.4 2.0 %collective-permute-start.4 = (f32[512,1024]{1,0:T(8,128)}, f32[512,1024]{1,0:T(8,128)}, u32[]{:S(2)}, u32[]{:S(2)}) collective-permute-start(f32[512,1024]{1,0:T(8,128)} %collective-permute-done.3.refs_1_), channel_id=1, source_target_pairs={{5,9},{26,22},{13,17},{18,14},{21,25},{10,6}} | collective-permute-start | bytes 6291464 | tf_op jit(solution)/shard_map/ppermute | solution.py:44
  35.4 1.0 pairs.7
  36.4 0.0 collective-permute-done.2.refs_2_
  36.4 2.1 %collective-permute-start.6 = (f32[512,1024]{1,0:T(8,128)}, f32[512,1024]{1,0:T(8,128)}, u32[]{:S(2)}, u32[]{:S(2)}) collective-permute-start(f32[512,1024]{1,0:T(8,128)} %bitcast.15), channel_id=1, source_target_pairs={{2,1},{29,30},{10,9},{21,22},{18,17},{13,14},{26,25},{5,6}} | collective-permute-start | bytes 6291464 | tf_op jit(solution)/shard_map/ppermute | solution.py:44
  38.5 2.0 %collective-permute-start.7 = (f32[512,1024]{1,0:T(8,128)}, f32[512,1024]{1,0:T(8,128)}, u32[]{:S(2)}, u32[]{:S(2)}) collective-permute-start(f32[512,1024]{1,0:T(8,128)} %collective-permute-done.2.refs_2_), channel_id=1, source_target_pairs={{5,9},{26,22},{13,17},{18,14},{21,25},{10,6}} | collective-permute-start | bytes 6291464 | tf_op jit(solution)/shard_map/ppermute | solution.py:44
  40.5 0.0 collective-permute-done.1.refs_1_.refs_0_
  40.5 0.0 collective-permute-done.4.refs_4_
  40.5 1.2 pairs.8
  41.7 2.0 %collective-permute-start.8 = (f32[512,1024]{1,0:T(8,128)}, f32[512,1024]{1,0:T(8,128)}, u32[]{:S(2)}, u32[]{:S(2)}) collective-permute-start(f32[512,1024]{1,0:T(8,128)} %collective-permute-done.6.refs_4_.refs_1_), channel_id=1, source_target_pairs={{1,5},{30,26},{9,13},{22,18},{17,21},{14,10},{25,29},{6,2}} | collective-permute-start | bytes 6291464 | tf_op jit(solution)/shard_map/ppermute | solution.py:44
  43.7 2.0 %collective-permute-start.5 = (f32[512,1024]{1,0:T(8,128)}, f32[512,1024]{1,0:T(8,128)}, u32[]{:S(2)}, u32[]{:S(2)}) collective-permute-start(f32[512,1024]{1,0:T(8,128)} %bitcast.17), channel_id=1, source_target_pairs={{3,5},{28,26},{11,13},{20,18},{19,21},{12,10},{27,29},{4,2}} | collective-permute-start | bytes 6291464 | tf_op jit(solution)/shard_map/ppermute | solution.py:44
  45.7 1.1 pairs.9
  46.8 1.3 collective-permute-start.14
  48.1 1.0 pairs.10.refs_2_
  49.1 0.0 collective-permute-done.5.refs_1_
  49.1 1.3 pairs.11
  50.4 2.1 %collective-permute-start.15 = (f32[512,1024]{1,0:T(8,128)}, f32[512,1024]{1,0:T(8,128)}, u32[]{:S(2)}, u32[]{:S(2)}) collective-permute-start(f32[512,1024]{1,0:T(8,128)} %get-tuple-element.52), channel_id=1, source_target_pairs={{5,4},{26,27},{13,12},{18,19},{21,20},{10,11},{29,28},{2,3}} | collective-permute-start | bytes 6291464 | tf_op jit(solution)/shard_map/ppermute | solution.py:44
  52.5 2.0 %collective-permute-start.9 = (f32[512,1024]{1,0:T(8,128)}, f32[512,1024]{1,0:T(8,128)}, u32[]{:S(2)}, u32[]{:S(2)}) collective-permute-start(f32[512,1024]{1,0:T(8,128)} %collective-permute-done.5.refs_1_), channel_id=1, source_target_pairs={{5,1},{26,30},{13,9},{18,22},{21,17},{10,14},{29,25},{2,6}} | collective-permute-start | bytes 6291464 | tf_op jit(solution)/shard_map/ppermute | solution.py:44
  54.5 2.5 %count.1 = f32[512,512]{1,0:T(8,128)} custom-call(f32[512,512]{1,0:T(8,128)} %get-tuple-element.54.density_ref), custom_call_target="tpu_custom_call" | custom-call | flops 1000 | bytes 1000 | tf_op jit(solution)/shard_map/count/pallas_call | solution.py:388
  57.0 1.1 dynamic-slice_bitcast_fusion
  58.1 61.1 %collective-permute-start.10 = (f32[4,64,512]{2,1,0:T(8,128)S(1)}, f32[4,64,512]{2,1,0:T(8,128)S(1)}, u32[]{:S(2)}, u32[]{:S(2)}) collective-permute-start(f32[4,64,512]{2,1,0:T(8,128)S(1)} %dynamic-slice_bitcast_fusion), channel_id=1, source_target_pairs={{0,4},{4,0},{8,12},{12,8},{16,20},{20,16},{24,28},{28,24},{1,5},{5... | collective-permute-start | bytes 1572872 | tf_op jit(solution)/shard_map/ppermute | solution.py:438
  119.1 1.5 collective-permute-done.10
  120.7 1.1 bitcast_add_fusion
  121.8 1.6 collective-permute-start.11
  123.4 1.5 collective-permute-start.12
  124.9 2.8 %collective-permute-done.11 = f32[1,64,512]{2,1,0:T(8,128)S(1)} collective-permute-done((f32[1,64,512]{2,1,0:T(8,128)S(1)}, f32[1,64,512]{2,1,0:T(8,128)S(1)}, u32[]{:S(2)}, u32[]{:S(2)}) %collective-permute-start.11) | collective-permute-done | bytes 131104 | tf_op jit(solution)/shard_map/ppermute | solution.py:438
  127.7 2.4 %collective-permute-start.13 = (f32[1,64,512]{2,1,0:T(8,128)S(1)}, f32[1,64,512]{2,1,0:T(8,128)S(1)}, u32[]{:S(2)}, u32[]{:S(2)}) collective-permute-start(f32[1,64,512]{2,1,0:T(8,128)S(1)} %get-tuple-element.61), channel_id=1, source_target_pairs={{0,24},{4,28},{8,16},{12,20},{16,8},{20,12},{24,0},{28,4},{1,25},{... | collective-permute-start | bytes 393224 | tf_op jit(solution)/shard_map/ppermute | solution.py:438
  130.1 0.0 collective-permute-done.12
  130.1 3.4 %collective-permute-done.13 = f32[1,64,512]{2,1,0:T(8,128)S(1)} collective-permute-done((f32[1,64,512]{2,1,0:T(8,128)S(1)}, f32[1,64,512]{2,1,0:T(8,128)S(1)}, u32[]{:S(2)}, u32[]{:S(2)}) %collective-permute-start.13) | collective-permute-done | bytes 131104 | tf_op jit(solution)/shard_map/ppermute | solution.py:438
  133.6 13.3 %collective-permute-start.16 = (f32[64,512]{1,0:T(8,128)S(1)}, f32[64,512]{1,0:T(8,128)S(1)}, u32[]{:S(2)}, u32[]{:S(2)}) collective-permute-start(f32[64,512]{1,0:T(8,128)S(1)} %add_bitcast_fusion), channel_id=1, source_target_pairs={{0,1},{1,0},{2,3},{3,2},{4,5},{5,4},{6,7},{7,6},{8,9},{9,8},{10,11... | collective-permute-start | bytes 393224 | tf_op jit(solution)/shard_map/ppermute | solution.py:443
  146.9 1.0 collective-permute-start.17
  147.9 1.5 collective-permute-start.18
  149.3 1.0 pairs.12.own_ref
  150.4 0.0 collective-permute-done.15.early_ref
  150.4 4.0 %home_sum.1.refs_2_ = f32[512,1024]{1,0:T(8,128)} custom-call(f32[32]{0:T(128)} %energy_ref.17, s32[32,2]{1,0:T(8,128)} %copy.26.mask_ref, f32[512,1024]{1,0:T(8,128)} %pairs.12.own_ref, f32[512,1024]{1,0:T(8,128)} %collective-permute-done.14.late_ref, f32[512,1024]{1,0:T(8,128)} %collective-permute-done.15.early_ref), custom_call_target="tpu_custom_call", output_to_operand_aliasing={{}: (2, {})} | custom-call | flops 1000 | bytes 1000 | tf_op jit(solution)/shard_map/home_sum/pallas_call | solution.py:396
  154.4 0.0 collective-permute-done.9.refs_1_
  154.4 1.0 pairs.13
  155.5 0.0 collective-permute-done.16
  155.5 2.7 %collective-permute-done.17 = f32[64,512]{1,0:T(8,128)S(1)} collective-permute-done((f32[64,512]{1,0:T(8,128)S(1)}, f32[64,512]{1,0:T(8,128)S(1)}, u32[]{:S(2)}, u32[]{:S(2)}) %collective-permute-start.17) | collective-permute-done | bytes 131104 | tf_op jit(solution)/shard_map/ppermute | solution.py:443
  158.2 0.0 collective-permute-done.18
  158.2 0.7 add_multiply_fusion
  (6 shorter events, 0.1 us)
Async XLA Ops:
  0.6 28.8 %collective-permute-start = (f32[512,1024]{1,0:T(8,128)}, f32[512,1024]{1,0:T(8,128)}, u32[]{:S(2)}, u32[]{:S(2)}) collective-permute-start(f32[512,1024]{1,0:T(8,128)} %bitcast.10), channel_id=1, source_target_pairs={{0,1},{31,30},{8,9},{23,22},{16,17},{15,14},{24,25},{7,6}} | collective-permute-start | bytes 6291464 | tf_op jit(solution)/shard_map/ppermute | solution.py:44
  6.9 24.5 %collective-permute-start.3 = (f32[512,1024]{1,0:T(8,128)}, f32[512,1024]{1,0:T(8,128)}, u32[]{:S(2)}, u32[]{:S(2)}) collective-permute-start(f32[512,1024]{1,0:T(8,128)} %bitcast.11), channel_id=1, source_target_pairs={{6,5},{25,26},{14,13},{17,18},{22,21},{9,10},{30,29},{1,2}} | collective-permute-start | bytes 6291464 | tf_op jit(solution)/shard_map/ppermute | solution.py:44
  29.4 7.0 %collective-permute-start.2 = (f32[512,1024]{1,0:T(8,128)}, f32[512,1024]{1,0:T(8,128)}, u32[]{:S(2)}, u32[]{:S(2)}) collective-permute-start(f32[512,1024]{1,0:T(8,128)} %collective-permute-done.refs_2_.refs_3_), channel_id=1, source_target_pairs={{6,5},{25,26},{14,13},{17,18},{22,21},{9,10},{30,29},{1,2}} | collective-permute-start | bytes 6291464 | tf_op jit(solution)/shard_map/ppermute | solution.py:44
  31.4 9.1 %collective-permute-start.1 = (f32[512,1024]{1,0:T(8,128)}, f32[512,1024]{1,0:T(8,128)}, u32[]{:S(2)}, u32[]{:S(2)}) collective-permute-start(f32[512,1024]{1,0:T(8,128)} %bitcast.13), channel_id=1, source_target_pairs={{4,5},{27,26},{12,13},{19,18},{20,21},{11,10},{28,29},{3,2}} | collective-permute-start | bytes 6291464 | tf_op jit(solution)/shard_map/ppermute | solution.py:44
  33.4 7.1 %collective-permute-start.4 = (f32[512,1024]{1,0:T(8,128)}, f32[512,1024]{1,0:T(8,128)}, u32[]{:S(2)}, u32[]{:S(2)}) collective-permute-start(f32[512,1024]{1,0:T(8,128)} %collective-permute-done.3.refs_1_), channel_id=1, source_target_pairs={{5,9},{26,22},{13,17},{18,14},{21,25},{10,6}} | collective-permute-start | bytes 6291464 | tf_op jit(solution)/shard_map/ppermute | solution.py:44
  36.4 5.3 %collective-permute-start.6 = (f32[512,1024]{1,0:T(8,128)}, f32[512,1024]{1,0:T(8,128)}, u32[]{:S(2)}, u32[]{:S(2)}) collective-permute-start(f32[512,1024]{1,0:T(8,128)} %bitcast.15), channel_id=1, source_target_pairs={{2,1},{29,30},{10,9},{21,22},{18,17},{13,14},{26,25},{5,6}} | collective-permute-start | bytes 6291464 | tf_op jit(solution)/shard_map/ppermute | solution.py:44
  38.5 7.2 %collective-permute-start.7 = (f32[512,1024]{1,0:T(8,128)}, f32[512,1024]{1,0:T(8,128)}, u32[]{:S(2)}, u32[]{:S(2)}) collective-permute-start(f32[512,1024]{1,0:T(8,128)} %collective-permute-done.2.refs_2_), channel_id=1, source_target_pairs={{5,9},{26,22},{13,17},{18,14},{21,25},{10,6}} | collective-permute-start | bytes 6291464 | tf_op jit(solution)/shard_map/ppermute | solution.py:44
  41.7 4.0 %collective-permute-start.8 = (f32[512,1024]{1,0:T(8,128)}, f32[512,1024]{1,0:T(8,128)}, u32[]{:S(2)}, u32[]{:S(2)}) collective-permute-start(f32[512,1024]{1,0:T(8,128)} %collective-permute-done.6.refs_4_.refs_1_), channel_id=1, source_target_pairs={{1,5},{30,26},{9,13},{22,18},{17,21},{14,10},{25,29},{6,2}} | collective-permute-start | bytes 6291464 | tf_op jit(solution)/shard_map/ppermute | solution.py:44
  43.7 5.4 %collective-permute-start.5 = (f32[512,1024]{1,0:T(8,128)}, f32[512,1024]{1,0:T(8,128)}, u32[]{:S(2)}, u32[]{:S(2)}) collective-permute-start(f32[512,1024]{1,0:T(8,128)} %bitcast.17), channel_id=1, source_target_pairs={{3,5},{28,26},{11,13},{20,18},{19,21},{12,10},{27,29},{4,2}} | collective-permute-start | bytes 6291464 | tf_op jit(solution)/shard_map/ppermute | solution.py:44
  46.8 86.8 %collective-permute-start.14 = (f32[512,1024]{1,0:T(8,128)}, f32[512,1024]{1,0:T(8,128)}, u32[]{:S(2)}, u32[]{:S(2)}) collective-permute-start(f32[512,1024]{1,0:T(8,128)} %get-tuple-element.48.refs_2_), channel_id=1, source_target_pairs={{1,0},{30,31},{9,8},{22,23},{17,16},{14,15},{25,24},{6,7}} | collective-permute-start | bytes 6291464 | tf_op jit(solution)/shard_map/ppermute | solution.py:44
  50.4 100.0 %collective-permute-start.15 = (f32[512,1024]{1,0:T(8,128)}, f32[512,1024]{1,0:T(8,128)}, u32[]{:S(2)}, u32[]{:S(2)}) collective-permute-start(f32[512,1024]{1,0:T(8,128)} %get-tuple-element.52), channel_id=1, source_target_pairs={{5,4},{26,27},{13,12},{18,19},{21,20},{10,11},{29,28},{2,3}} | collective-permute-start | bytes 6291464 | tf_op jit(solution)/shard_map/ppermute | solution.py:44
  52.5 102.0 %collective-permute-start.9 = (f32[512,1024]{1,0:T(8,128)}, f32[512,1024]{1,0:T(8,128)}, u32[]{:S(2)}, u32[]{:S(2)}) collective-permute-start(f32[512,1024]{1,0:T(8,128)} %collective-permute-done.5.refs_1_), channel_id=1, source_target_pairs={{5,1},{26,30},{13,9},{18,22},{21,17},{10,14},{29,25},{2,6}} | collective-permute-start | bytes 6291464 | tf_op jit(solution)/shard_map/ppermute | solution.py:44
  58.1 62.6 %collective-permute-start.10 = (f32[4,64,512]{2,1,0:T(8,128)S(1)}, f32[4,64,512]{2,1,0:T(8,128)S(1)}, u32[]{:S(2)}, u32[]{:S(2)}) collective-permute-start(f32[4,64,512]{2,1,0:T(8,128)S(1)} %dynamic-slice_bitcast_fusion), channel_id=1, source_target_pairs={{0,4},{4,0},{8,12},{12,8},{16,20},{20,16},{24,28},{28,24},{1,5},{5... | collective-permute-start | bytes 1572872 | tf_op jit(solution)/shard_map/ppermute | solution.py:438
  121.8 5.8 %collective-permute-start.11 = (f32[1,64,512]{2,1,0:T(8,128)S(1)}, f32[1,64,512]{2,1,0:T(8,128)S(1)}, u32[]{:S(2)}, u32[]{:S(2)}) collective-permute-start(f32[1,64,512]{2,1,0:T(8,128)S(1)} %get-tuple-element.60), channel_id=1, source_target_pairs={{0,8},{4,12},{8,0},{12,4},{16,24},{20,28},{24,16},{28,20},{1,9},{5... | collective-permute-start | bytes 393224 | tf_op jit(solution)/shard_map/ppermute | solution.py:438
  123.4 6.7 %collective-permute-start.12 = (f32[1,64,512]{2,1,0:T(8,128)S(1)}, f32[1,64,512]{2,1,0:T(8,128)S(1)}, u32[]{:S(2)}, u32[]{:S(2)}) collective-permute-start(f32[1,64,512]{2,1,0:T(8,128)S(1)} %get-tuple-element.62), channel_id=1, source_target_pairs={{0,16},{4,20},{8,24},{12,28},{16,0},{20,4},{24,8},{28,12},{1,17},{... | collective-permute-start | bytes 393224 | tf_op jit(solution)/shard_map/ppermute | solution.py:438
  127.7 5.9 %collective-permute-start.13 = (f32[1,64,512]{2,1,0:T(8,128)S(1)}, f32[1,64,512]{2,1,0:T(8,128)S(1)}, u32[]{:S(2)}, u32[]{:S(2)}) collective-permute-start(f32[1,64,512]{2,1,0:T(8,128)S(1)} %get-tuple-element.61), channel_id=1, source_target_pairs={{0,24},{4,28},{8,16},{12,20},{16,8},{20,12},{24,0},{28,4},{1,25},{... | collective-permute-start | bytes 393224 | tf_op jit(solution)/shard_map/ppermute | solution.py:438
  133.6 21.9 %collective-permute-start.16 = (f32[64,512]{1,0:T(8,128)S(1)}, f32[64,512]{1,0:T(8,128)S(1)}, u32[]{:S(2)}, u32[]{:S(2)}) collective-permute-start(f32[64,512]{1,0:T(8,128)S(1)} %add_bitcast_fusion), channel_id=1, source_target_pairs={{0,1},{1,0},{2,3},{3,2},{4,5},{5,4},{6,7},{7,6},{8,9},{9,8},{10,11... | collective-permute-start | bytes 393224 | tf_op jit(solution)/shard_map/ppermute | solution.py:443
  146.9 11.3 %collective-permute-start.17 = (f32[64,512]{1,0:T(8,128)S(1)}, f32[64,512]{1,0:T(8,128)S(1)}, u32[]{:S(2)}, u32[]{:S(2)}) collective-permute-start(f32[64,512]{1,0:T(8,128)S(1)} %add_bitcast_fusion), channel_id=1, source_target_pairs={{0,2},{1,3},{2,0},{3,1},{4,6},{5,7},{6,4},{7,5},{8,10},{9,11},{10,... | collective-permute-start | bytes 393224 | tf_op jit(solution)/shard_map/ppermute | solution.py:443
  147.9 10.3 %collective-permute-start.18 = (f32[64,512]{1,0:T(8,128)S(1)}, f32[64,512]{1,0:T(8,128)S(1)}, u32[]{:S(2)}, u32[]{:S(2)}) collective-permute-start(f32[64,512]{1,0:T(8,128)S(1)} %add_bitcast_fusion), channel_id=1, source_target_pairs={{0,3},{1,2},{2,1},{3,0},{4,7},{5,6},{6,5},{7,4},{8,11},{9,10},{10,... | collective-permute-start | bytes 393224 | tf_op jit(solution)/shard_map/ppermute | solution.py:443
where the time goes:
time: 162 us; the launch traced here: 159 us
  starting transfers between devices  110 us (68%)
  waiting for transfers between devices  22.3 us (14%)
  Pallas kernels  21.5 us (13%)
  local copies, waits for them, and re-layouts  2.48 us (2%)
  other arithmetic  1.85 us (1%)
    ppermute x4, starting transfers between devices, reduced(): part = lax.ppermute(part, 'occ', [(o, o ^ j * bit) for o in range(nocc)])  66.6 us
    ppermute x12, starting transfers between devices, move(): return lax.ppermute(block, AXES, route)  27.6 us
    ppermute x3, starting transfers between devices, reduced(): lax.ppermute(blocks, 'grp', [(g, g ^ j) for g in range(ngrp)])  15.7 us
    ppermute x12, waiting for transfers between devices, move(): return lax.ppermute(block, AXES, route)  11.9 us
    ppermute x4, waiting for transfers between devices, reduced(): part = lax.ppermute(part, 'occ', [(o, o ^ j * bit) for o in range(nocc)])  7.71 us
    pallas_call x7, Pallas kernels, pairs(): pl.pallas_call(functools.partial(pairs_kernel, nocc, tasks, list(there),...  7.66 us
    pallas_call x1, Pallas kernels, body(): pl.pallas_call(functools.partial(home_kernel, nocc), out_shape=[slab, squ...  7.27 us
    pallas_call x1, Pallas kernels, meanwhile(): pl.pallas_call(functools.partial(home_sum_kernel, nocc), out_shape=slab,...  4.05 us
  transfers between devices with their start and end apart: 19, of which 5 were waited for; matrix products, arithmetic and copies ran while one was open for 2% of the time, Pallas kernels for 14%

commit v1 on v0

--- a/solution.py
+++ b/solution.py
@@ -359,7 +359,7 @@
             ("early", "a0", "a2", "g0", "", "all"),
             ("early", "a0", "p2", "g0", "", "all"),
             ("late", "a0", "a2", "g0", "", ""),
-            ("late", "a0", "p3", "g0", "", "lower"),
+            ("late", "a0", "p3", "g0", "", ""),
         ],
         {
             "early0": early0, "early2": early2, "early_p2": early_p2, "late0": late0, "late2": late2,
@@ -369,11 +369,15 @@
         ["g0", "density"],
     )
     late_home = move(g0, routes["late_home"])
-    (g1,) = pairs(
-        [("late", "a1", "a2", "g1", "", ""), ("late", "a1", "p3", "g1", "", "")],
-        {"own": own, "late2": late2, "late_p3": late_p3},
-        {"g1": tied(g1, g0)},
-        ["g1"],
+    g1, density = pairs(
+        [
+            ("late", "a1", "a2", "g1", "", ""),
+            ("late", "a1", "p3", "g1", "", ""),
+            ("late", "a0", "p3", "", "", "lower"),
+        ],
+        {"own": own, "late0": late0, "late2": late2, "late_p3": late_p3},
+        {"g1": tied(g1, g0), "density": density},
+        ["g1", "density"],
     )
     early_p3 = tied(early_p3, g1)
     g0, density = pairs(

time: 162 us -> 161 us (level)
  no operation moved by 1% of the time
where the time goes in v1:
time: 161 us; the launch traced here: 159 us
  starting transfers between devices  110 us (68%)
  waiting for transfers between devices  22.5 us (14%)
  Pallas kernels  21.5 us (13%)
  local copies, waits for them, and re-layouts  2.48 us (2%)
  other arithmetic  1.85 us (1%)
    ppermute x4, starting transfers between devices, reduced(): part = lax.ppermute(part, 'occ', [(o, o ^ j * bit) for o in range(nocc)])  66.3 us
    ppermute x12, starting transfers between devices, move(): return lax.ppermute(block, AXES, route)  27.7 us
    ppermute x3, starting transfers between devices, reduced(): lax.ppermute(blocks, 'grp', [(g, g ^ j) for g in range(ngrp)])  15.6 us
    ppermute x12, waiting for transfers between devices, move(): return lax.ppermute(block, AXES, route)  11.9 us
    ppermute x4, waiting for transfers between devices, reduced(): part = lax.ppermute(part, 'occ', [(o, o ^ j * bit) for o in range(nocc)])  7.8 us
    pallas_call x7, Pallas kernels, pairs(): pl.pallas_call(functools.partial(pairs_kernel, nocc, tasks, list(there),...  7.64 us
    pallas_call x1, Pallas kernels, body(): pl.pallas_call(functools.partial(home_kernel, nocc), out_shape=[slab, squ...  7.27 us
    pallas_call x1, Pallas kernels, meanwhile(): pl.pallas_call(functools.partial(home_sum_kernel, nocc), out_shape=slab,...  4.05 us
  transfers between devices with their start and end apart: 19, of which 5 were waited for; matrix products, arithmetic and copies ran while one was open for 2% of the time, Pallas kernels for 14%

profile of v1, /device:TPU:0, one launch (start us, length us, event | category | flops | bytes accessed | tf_op | source)
XLA Modules:
  0.0 158.7 jit_solution(16330529091578502257)
XLA Ops:
  0.6 6.2 %collective-permute-start = (f32[512,1024]{1,0:T(8,128)}, f32[512,1024]{1,0:T(8,128)}, u32[]{:S(2)}, u32[]{:S(2)}) collective-permute-start(f32[512,1024]{1,0:T(8,128)} %bitcast.10), channel_id=1, source_target_pairs={{0,1},{31,30},{8,9},{23,22},{16,17},{15,14},{24,25},{7,6}} | collective-permute-start | bytes 6291464 | tf_op jit(solution)/shard_map/ppermute | solution.py:44
  6.9 2.0 %collective-permute-start.3 = (f32[512,1024]{1,0:T(8,128)}, f32[512,1024]{1,0:T(8,128)}, u32[]{:S(2)}, u32[]{:S(2)}) collective-permute-start(f32[512,1024]{1,0:T(8,128)} %bitcast.11), channel_id=1, source_target_pairs={{6,5},{25,26},{14,13},{17,18},{22,21},{9,10},{30,29},{1,2}} | collective-permute-start | bytes 6291464 | tf_op jit(solution)/shard_map/ppermute | solution.py:44
  8.9 1.4 copy.27.mask_ref
  10.3 7.3 %home_pair.1 = (f32[512,1024]{1,0:T(8,128)}, f32[512,512]{1,0:T(8,128)}, f32[512,512]{1,0:T(8,128)}) custom-call(f32[32]{0:T(128)} %energy_ref.17, s32[32,2]{1,0:T(8,128)} %copy.27.mask_ref, f32[1,512]{1,0:T(1,128)} %bitcast.24, f32[512,1024]{1,0:T(8,128)} %bitcast.12), custom_call_target="tpu_custom_call" | custom-call | flops 1000 | bytes 1000 | tf_op jit(solution)/shard_map/home_pair/pallas_call | solution.py:322
  17.5 11.9 %collective-permute-done.refs_2_.refs_3_.refs_1_ = f32[512,1024]{1,0:T(8,128)} collective-permute-done((f32[512,1024]{1,0:T(8,128)}, f32[512,1024]{1,0:T(8,128)}, u32[]{:S(2)}, u32[]{:S(2)}) %collective-permute-start) | collective-permute-done | bytes 2097184 | tf_op jit(solution)/shard_map/ppermute | solution.py:44
  29.4 2.0 %collective-permute-start.2 = (f32[512,1024]{1,0:T(8,128)}, f32[512,1024]{1,0:T(8,128)}, u32[]{:S(2)}, u32[]{:S(2)}) collective-permute-start(f32[512,1024]{1,0:T(8,128)} %collective-permute-done.refs_2_.refs_3_.refs_1_), channel_id=1, source_target_pairs={{6,5},{25,26},{14,13},{17,18},{22,21},{9,10},{30,29},{1,2}} | collective-permute-start | bytes 6291464 | tf_op jit(solution)/shard_map/ppermute | solution.py:44
  31.4 0.0 collective-permute-done.3.refs_1_
  31.4 2.0 %collective-permute-start.1 = (f32[512,1024]{1,0:T(8,128)}, f32[512,1024]{1,0:T(8,128)}, u32[]{:S(2)}, u32[]{:S(2)}) collective-permute-start(f32[512,1024]{1,0:T(8,128)} %bitcast.13), channel_id=1, source_target_pairs={{4,5},{27,26},{12,13},{19,18},{20,21},{11,10},{28,29},{3,2}} | collective-permute-start | bytes 6291464 | tf_op jit(solution)/shard_map/ppermute | solution.py:44
  33.4 2.0 %collective-permute-start.4 = (f32[512,1024]{1,0:T(8,128)}, f32[512,1024]{1,0:T(8,128)}, u32[]{:S(2)}, u32[]{:S(2)}) collective-permute-start(f32[512,1024]{1,0:T(8,128)} %collective-permute-done.3.refs_1_), channel_id=1, source_target_pairs={{5,9},{26,22},{13,17},{18,14},{21,25},{10,6}} | collective-permute-start | bytes 6291464 | tf_op jit(solution)/shard_map/ppermute | solution.py:44
  35.4 1.0 pairs.7
  36.4 0.0 collective-permute-done.2.refs_2_
  36.4 2.1 %collective-permute-start.6 = (f32[512,1024]{1,0:T(8,128)}, f32[512,1024]{1,0:T(8,128)}, u32[]{:S(2)}, u32[]{:S(2)}) collective-permute-start(f32[512,1024]{1,0:T(8,128)} %bitcast.15), channel_id=1, source_target_pairs={{2,1},{29,30},{10,9},{21,22},{18,17},{13,14},{26,25},{5,6}} | collective-permute-start | bytes 6291464 | tf_op jit(solution)/shard_map/ppermute | solution.py:44
  38.5 2.0 %collective-permute-start.7 = (f32[512,1024]{1,0:T(8,128)}, f32[512,1024]{1,0:T(8,128)}, u32[]{:S(2)}, u32[]{:S(2)}) collective-permute-start(f32[512,1024]{1,0:T(8,128)} %collective-permute-done.2.refs_2_), channel_id=1, source_target_pairs={{5,9},{26,22},{13,17},{18,14},{21,25},{10,6}} | collective-permute-start | bytes 6291464 | tf_op jit(solution)/shard_map/ppermute | solution.py:44
  40.5 0.0 collective-permute-done.1.refs_1_.refs_0_
  40.5 0.0 collective-permute-done.4.refs_4_
  40.5 1.2 pairs.8
  41.8 0.0 collective-permute-done.6.refs_4_.refs_2_
  41.8 2.0 %collective-permute-start.8 = (f32[512,1024]{1,0:T(8,128)}, f32[512,1024]{1,0:T(8,128)}, u32[]{:S(2)}, u32[]{:S(2)}) collective-permute-start(f32[512,1024]{1,0:T(8,128)} %collective-permute-done.6.refs_4_.refs_2_), channel_id=1, source_target_pairs={{1,5},{30,26},{9,13},{22,18},{17,21},{14,10},{25,29},{6,2}} | collective-permute-start | bytes 6291464 | tf_op jit(solution)/shard_map/ppermute | solution.py:44
  43.8 2.0 %collective-permute-start.5 = (f32[512,1024]{1,0:T(8,128)}, f32[512,1024]{1,0:T(8,128)}, u32[]{:S(2)}, u32[]{:S(2)}) collective-permute-start(f32[512,1024]{1,0:T(8,128)} %bitcast.17), channel_id=1, source_target_pairs={{3,5},{28,26},{11,13},{20,18},{19,21},{12,10},{27,29},{4,2}} | collective-permute-start | bytes 6291464 | tf_op jit(solution)/shard_map/ppermute | solution.py:44
  45.8 1.1 pairs.9
  46.8 1.3 collective-permute-start.14
  48.1 1.3 pairs.10
  49.4 0.0 collective-permute-done.5.refs_1_
  49.4 1.0 pairs.11
  50.5 2.1 %collective-permute-start.15 = (f32[512,1024]{1,0:T(8,128)}, f32[512,1024]{1,0:T(8,128)}, u32[]{:S(2)}, u32[]{:S(2)}) collective-permute-start(f32[512,1024]{1,0:T(8,128)} %get-tuple-element.56), channel_id=1, source_target_pairs={{5,4},{26,27},{13,12},{18,19},{21,20},{10,11},{29,28},{2,3}} | collective-permute-start | bytes 6291464 | tf_op jit(solution)/shard_map/ppermute | solution.py:44
  52.5 2.0 %collective-permute-start.9 = (f32[512,1024]{1,0:T(8,128)}, f32[512,1024]{1,0:T(8,128)}, u32[]{:S(2)}, u32[]{:S(2)}) collective-permute-start(f32[512,1024]{1,0:T(8,128)} %collective-permute-done.5.refs_1_), channel_id=1, source_target_pairs={{5,1},{26,30},{13,9},{18,22},{21,17},{10,14},{29,25},{2,6}} | collective-permute-start | bytes 6291464 | tf_op jit(solution)/shard_map/ppermute | solution.py:44
  54.5 2.6 %count.1 = f32[512,512]{1,0:T(8,128)} custom-call(f32[512,512]{1,0:T(8,128)} %get-tuple-element.58.density_ref), custom_call_target="tpu_custom_call" | custom-call | flops 1000 | bytes 1000 | tf_op jit(solution)/shard_map/count/pallas_call | solution.py:392
  57.1 1.1 dynamic-slice_bitcast_fusion
  58.2 60.7 %collective-permute-start.10 = (f32[4,64,512]{2,1,0:T(8,128)S(1)}, f32[4,64,512]{2,1,0:T(8,128)S(1)}, u32[]{:S(2)}, u32[]{:S(2)}) collective-permute-start(f32[4,64,512]{2,1,0:T(8,128)S(1)} %dynamic-slice_bitcast_fusion), channel_id=1, source_target_pairs={{0,4},{4,0},{8,12},{12,8},{16,20},{20,16},{24,28},{28,24},{1,5},{5... | collective-permute-start | bytes 1572872 | tf_op jit(solution)/shard_map/ppermute | solution.py:442
  118.9 1.5 collective-permute-done.10
  120.4 1.1 bitcast_add_fusion
  121.6 1.6 collective-permute-start.11
  123.2 1.5 collective-permute-start.12
  124.7 2.8 %collective-permute-done.11 = f32[1,64,512]{2,1,0:T(8,128)S(1)} collective-permute-done((f32[1,64,512]{2,1,0:T(8,128)S(1)}, f32[1,64,512]{2,1,0:T(8,128)S(1)}, u32[]{:S(2)}, u32[]{:S(2)}) %collective-permute-start.11) | collective-permute-done | bytes 131104 | tf_op jit(solution)/shard_map/ppermute | solution.py:442
  127.4 2.4 %collective-permute-start.13 = (f32[1,64,512]{2,1,0:T(8,128)S(1)}, f32[1,64,512]{2,1,0:T(8,128)S(1)}, u32[]{:S(2)}, u32[]{:S(2)}) collective-permute-start(f32[1,64,512]{2,1,0:T(8,128)S(1)} %get-tuple-element.65), channel_id=1, source_target_pairs={{0,24},{4,28},{8,16},{12,20},{16,8},{20,12},{24,0},{28,4},{1,25},{... | collective-permute-start | bytes 393224 | tf_op jit(solution)/shard_map/ppermute | solution.py:442
  129.9 3.5 %collective-permute-done.13 = f32[1,64,512]{2,1,0:T(8,128)S(1)} collective-permute-done((f32[1,64,512]{2,1,0:T(8,128)S(1)}, f32[1,64,512]{2,1,0:T(8,128)S(1)}, u32[]{:S(2)}, u32[]{:S(2)}) %collective-permute-start.13) | collective-permute-done | bytes 131104 | tf_op jit(solution)/shard_map/ppermute | solution.py:442
  133.4 0.0 collective-permute-done.14.late_ref
  133.4 13.2 %collective-permute-start.16 = (f32[64,512]{1,0:T(8,128)S(1)}, f32[64,512]{1,0:T(8,128)S(1)}, u32[]{:S(2)}, u32[]{:S(2)}) collective-permute-start(f32[64,512]{1,0:T(8,128)S(1)} %add_bitcast_fusion), channel_id=1, source_target_pairs={{0,1},{1,0},{2,3},{3,2},{4,5},{5,4},{6,7},{7,6},{8,9},{9,8},{10,11... | collective-permute-start | bytes 393224 | tf_op jit(solution)/shard_map/ppermute | solution.py:447
  146.6 0.5 collective-permute-start.17
  147.1 1.9 %collective-permute-start.18 = (f32[64,512]{1,0:T(8,128)S(1)}, f32[64,512]{1,0:T(8,128)S(1)}, u32[]{:S(2)}, u32[]{:S(2)}) collective-permute-start(f32[64,512]{1,0:T(8,128)S(1)} %add_bitcast_fusion), channel_id=1, source_target_pairs={{0,3},{1,2},{2,1},{3,0},{4,7},{5,6},{6,5},{7,4},{8,11},{9,10},{10,... | collective-permute-start | bytes 393224 | tf_op jit(solution)/shard_map/ppermute | solution.py:447
  149.0 1.0 pairs.12.own_ref
  150.1 0.0 collective-permute-done.15.early_ref
  150.1 4.0 %home_sum.1.refs_2_ = f32[512,1024]{1,0:T(8,128)} custom-call(f32[32]{0:T(128)} %energy_ref.17, s32[32,2]{1,0:T(8,128)} %copy.27.mask_ref, f32[512,1024]{1,0:T(8,128)} %pairs.12.own_ref, f32[512,1024]{1,0:T(8,128)} %collective-permute-done.14.late_ref, f32[512,1024]{1,0:T(8,128)} %collective-permute-done.15.early_ref), custom_call_target="tpu_custom_call", output_to_operand_aliasing={{}: (2, {})} | custom-call | flops 1000 | bytes 1000 | tf_op jit(solution)/shard_map/home_sum/pallas_call | solution.py:400
  154.1 0.0 collective-permute-done.9.refs_1_
  154.1 1.0 pairs.13
  155.2 2.8 %collective-permute-done.17 = f32[64,512]{1,0:T(8,128)S(1)} collective-permute-done((f32[64,512]{1,0:T(8,128)S(1)}, f32[64,512]{1,0:T(8,128)S(1)}, u32[]{:S(2)}, u32[]{:S(2)}) %collective-permute-start.17) | collective-permute-done | bytes 131104 | tf_op jit(solution)/shard_map/ppermute | solution.py:447
  158.0 0.0 collective-permute-done.18
  158.0 0.7 add_multiply_fusion
  (6 shorter events, 0.1 us)
Async XLA Ops:
  0.6 28.8 %collective-permute-start = (f32[512,1024]{1,0:T(8,128)}, f32[512,1024]{1,0:T(8,128)}, u32[]{:S(2)}, u32[]{:S(2)}) collective-permute-start(f32[512,1024]{1,0:T(8,128)} %bitcast.10), channel_id=1, source_target_pairs={{0,1},{31,30},{8,9},{23,22},{16,17},{15,14},{24,25},{7,6}} | collective-permute-start | bytes 6291464 | tf_op jit(solution)/shard_map/ppermute | solution.py:44
  6.9 24.5 %collective-permute-start.3 = (f32[512,1024]{1,0:T(8,128)}, f32[512,1024]{1,0:T(8,128)}, u32[]{:S(2)}, u32[]{:S(2)}) collective-permute-start(f32[512,1024]{1,0:T(8,128)} %bitcast.11), channel_id=1, source_target_pairs={{6,5},{25,26},{14,13},{17,18},{22,21},{9,10},{30,29},{1,2}} | collective-permute-start | bytes 6291464 | tf_op jit(solution)/shard_map/ppermute | solution.py:44
  29.4 7.0 %collective-permute-start.2 = (f32[512,1024]{1,0:T(8,128)}, f32[512,1024]{1,0:T(8,128)}, u32[]{:S(2)}, u32[]{:S(2)}) collective-permute-start(f32[512,1024]{1,0:T(8,128)} %collective-permute-done.refs_2_.refs_3_.refs_1_), channel_id=1, source_target_pairs={{6,5},{25,26},{14,13},{17,18},{22,21},{9,10},{30,29},{1,2}} | collective-permute-start | bytes 6291464 | tf_op jit(solution)/shard_map/ppermute | solution.py:44
  31.4 9.1 %collective-permute-start.1 = (f32[512,1024]{1,0:T(8,128)}, f32[512,1024]{1,0:T(8,128)}, u32[]{:S(2)}, u32[]{:S(2)}) collective-permute-start(f32[512,1024]{1,0:T(8,128)} %bitcast.13), channel_id=1, source_target_pairs={{4,5},{27,26},{12,13},{19,18},{20,21},{11,10},{28,29},{3,2}} | collective-permute-start | bytes 6291464 | tf_op jit(solution)/shard_map/ppermute | solution.py:44
  33.4 7.1 %collective-permute-start.4 = (f32[512,1024]{1,0:T(8,128)}, f32[512,1024]{1,0:T(8,128)}, u32[]{:S(2)}, u32[]{:S(2)}) collective-permute-start(f32[512,1024]{1,0:T(8,128)} %collective-permute-done.3.refs_1_), channel_id=1, source_target_pairs={{5,9},{26,22},{13,17},{18,14},{21,25},{10,6}} | collective-permute-start | bytes 6291464 | tf_op jit(solution)/shard_map/ppermute | solution.py:44
  36.4 5.3 %collective-permute-start.6 = (f32[512,1024]{1,0:T(8,128)}, f32[512,1024]{1,0:T(8,128)}, u32[]{:S(2)}, u32[]{:S(2)}) collective-permute-start(f32[512,1024]{1,0:T(8,128)} %bitcast.15), channel_id=1, source_target_pairs={{2,1},{29,30},{10,9},{21,22},{18,17},{13,14},{26,25},{5,6}} | collective-permute-start | bytes 6291464 | tf_op jit(solution)/shard_map/ppermute | solution.py:44
  38.5 7.3 %collective-permute-start.7 = (f32[512,1024]{1,0:T(8,128)}, f32[512,1024]{1,0:T(8,128)}, u32[]{:S(2)}, u32[]{:S(2)}) collective-permute-start(f32[512,1024]{1,0:T(8,128)} %collective-permute-done.2.refs_2_), channel_id=1, source_target_pairs={{5,9},{26,22},{13,17},{18,14},{21,25},{10,6}} | collective-permute-start | bytes 6291464 | tf_op jit(solution)/shard_map/ppermute | solution.py:44
  41.8 4.0 %collective-permute-start.8 = (f32[512,1024]{1,0:T(8,128)}, f32[512,1024]{1,0:T(8,128)}, u32[]{:S(2)}, u32[]{:S(2)}) collective-permute-start(f32[512,1024]{1,0:T(8,128)} %collective-permute-done.6.refs_4_.refs_2_), channel_id=1, source_target_pairs={{1,5},{30,26},{9,13},{22,18},{17,21},{14,10},{25,29},{6,2}} | collective-permute-start | bytes 6291464 | tf_op jit(solution)/shard_map/ppermute | solution.py:44
  43.8 5.7 %collective-permute-start.5 = (f32[512,1024]{1,0:T(8,128)}, f32[512,1024]{1,0:T(8,128)}, u32[]{:S(2)}, u32[]{:S(2)}) collective-permute-start(f32[512,1024]{1,0:T(8,128)} %bitcast.17), channel_id=1, source_target_pairs={{3,5},{28,26},{11,13},{20,18},{19,21},{12,10},{27,29},{4,2}} | collective-permute-start | bytes 6291464 | tf_op jit(solution)/shard_map/ppermute | solution.py:44
  46.8 86.6 %collective-permute-start.14 = (f32[512,1024]{1,0:T(8,128)}, f32[512,1024]{1,0:T(8,128)}, u32[]{:S(2)}, u32[]{:S(2)}) collective-permute-start(f32[512,1024]{1,0:T(8,128)} %get-tuple-element.50.refs_2_), channel_id=1, source_target_pairs={{1,0},{30,31},{9,8},{22,23},{17,16},{14,15},{25,24},{6,7}} | collective-permute-start | bytes 6291464 | tf_op jit(solution)/shard_map/ppermute | solution.py:44
  50.5 99.6 %collective-permute-start.15 = (f32[512,1024]{1,0:T(8,128)}, f32[512,1024]{1,0:T(8,128)}, u32[]{:S(2)}, u32[]{:S(2)}) collective-permute-start(f32[512,1024]{1,0:T(8,128)} %get-tuple-element.56), channel_id=1, source_target_pairs={{5,4},{26,27},{13,12},{18,19},{21,20},{10,11},{29,28},{2,3}} | collective-permute-start | bytes 6291464 | tf_op jit(solution)/shard_map/ppermute | solution.py:44
  52.5 101.6 %collective-permute-start.9 = (f32[512,1024]{1,0:T(8,128)}, f32[512,1024]{1,0:T(8,128)}, u32[]{:S(2)}, u32[]{:S(2)}) collective-permute-start(f32[512,1024]{1,0:T(8,128)} %collective-permute-done.5.refs_1_), channel_id=1, source_target_pairs={{5,1},{26,30},{13,9},{18,22},{21,17},{10,14},{29,25},{2,6}} | collective-permute-start | bytes 6291464 | tf_op jit(solution)/shard_map/ppermute | solution.py:44
  58.2 62.3 %collective-permute-start.10 = (f32[4,64,512]{2,1,0:T(8,128)S(1)}, f32[4,64,512]{2,1,0:T(8,128)S(1)}, u32[]{:S(2)}, u32[]{:S(2)}) collective-permute-start(f32[4,64,512]{2,1,0:T(8,128)S(1)} %dynamic-slice_bitcast_fusion), channel_id=1, source_target_pairs={{0,4},{4,0},{8,12},{12,8},{16,20},{20,16},{24,28},{28,24},{1,5},{5... | collective-permute-start | bytes 1572872 | tf_op jit(solution)/shard_map/ppermute | solution.py:442
  121.6 5.8 %collective-permute-start.11 = (f32[1,64,512]{2,1,0:T(8,128)S(1)}, f32[1,64,512]{2,1,0:T(8,128)S(1)}, u32[]{:S(2)}, u32[]{:S(2)}) collective-permute-start(f32[1,64,512]{2,1,0:T(8,128)S(1)} %get-tuple-element.64), channel_id=1, source_target_pairs={{0,8},{4,12},{8,0},{12,4},{16,24},{20,28},{24,16},{28,20},{1,9},{5... | collective-permute-start | bytes 393224 | tf_op jit(solution)/shard_map/ppermute | solution.py:442
  123.2 6.7 %collective-permute-start.12 = (f32[1,64,512]{2,1,0:T(8,128)S(1)}, f32[1,64,512]{2,1,0:T(8,128)S(1)}, u32[]{:S(2)}, u32[]{:S(2)}) collective-permute-start(f32[1,64,512]{2,1,0:T(8,128)S(1)} %get-tuple-element.66), channel_id=1, source_target_pairs={{0,16},{4,20},{8,24},{12,28},{16,0},{20,4},{24,8},{28,12},{1,17},{... | collective-permute-start | bytes 393224 | tf_op jit(solution)/shard_map/ppermute | solution.py:442
  127.4 6.0 %collective-permute-start.13 = (f32[1,64,512]{2,1,0:T(8,128)S(1)}, f32[1,64,512]{2,1,0:T(8,128)S(1)}, u32[]{:S(2)}, u32[]{:S(2)}) collective-permute-start(f32[1,64,512]{2,1,0:T(8,128)S(1)} %get-tuple-element.65), channel_id=1, source_target_pairs={{0,24},{4,28},{8,16},{12,20},{16,8},{20,12},{24,0},{28,4},{1,25},{... | collective-permute-start | bytes 393224 | tf_op jit(solution)/shard_map/ppermute | solution.py:442
  133.4 21.7 %collective-permute-start.16 = (f32[64,512]{1,0:T(8,128)S(1)}, f32[64,512]{1,0:T(8,128)S(1)}, u32[]{:S(2)}, u32[]{:S(2)}) collective-permute-start(f32[64,512]{1,0:T(8,128)S(1)} %add_bitcast_fusion), channel_id=1, source_target_pairs={{0,1},{1,0},{2,3},{3,2},{4,5},{5,4},{6,7},{7,6},{8,9},{9,8},{10,11... | collective-permute-start | bytes 393224 | tf_op jit(solution)/shard_map/ppermute | solution.py:447
  146.6 11.4 %collective-permute-start.17 = (f32[64,512]{1,0:T(8,128)S(1)}, f32[64,512]{1,0:T(8,128)S(1)}, u32[]{:S(2)}, u32[]{:S(2)}) collective-permute-start(f32[64,512]{1,0:T(8,128)S(1)} %add_bitcast_fusion), channel_id=1, source_target_pairs={{0,2},{1,3},{2,0},{3,1},{4,6},{5,7},{6,4},{7,5},{8,10},{9,11},{10,... | collective-permute-start | bytes 393224 | tf_op jit(solution)/shard_map/ppermute | solution.py:447
  147.1 10.8 %collective-permute-start.18 = (f32[64,512]{1,0:T(8,128)S(1)}, f32[64,512]{1,0:T(8,128)S(1)}, u32[]{:S(2)}, u32[]{:S(2)}) collective-permute-start(f32[64,512]{1,0:T(8,128)S(1)} %add_bitcast_fusion), channel_id=1, source_target_pairs={{0,3},{1,2},{2,1},{3,0},{4,7},{5,6},{6,5},{7,4},{8,11},{9,10},{10,... | collective-permute-start | bytes 393224 | tf_op jit(solution)/shard_map/ppermute | solution.py:447
